TPU v7x, 128 devices: a whole 4x4x4 slice. The times are simulated.
128 devices in a mesh: seq: 2 (over y_hi), dp: 64 (over y_lo, z, x, core).
Axes of the slice: x: 4, y: 4 (y_hi: 2, y_lo: 2; y = y_hi * 2 + y_lo), z: 4, core: 2. Of those that a mesh axis runs over, the one named last changes fastest.
Arguments:
- tokens: bfloat16 [65536, 768], P(('seq', 'dp')), may hold values from -6 to 6
- input_weight: bfloat16 [768, 2304], replicated, may hold values from -0.21875 to 0.21875
- query_bias: float32 [768], replicated, may hold values from -3 to 3
- value_bias: float32 [768], replicated, may hold values from -1.2 to 1.2
- out_weight: bfloat16 [768, 768], replicated, may hold values from -1.75 to 1.75
- out_bias: float32 [768], replicated, may hold values from -2 to 2
- first_gain: float32 [768], replicated, may hold values from 0.5 to 1.5
- first_shift: float32 [768], replicated, may hold values from -2 to 2
- second_gain: float32 [768], replicated, may hold values from 0.5 to 1.5
- second_shift: float32 [768], replicated, may hold values from -2 to 2
- up_weight: bfloat16 [768, 3072], replicated, may hold values from -0.21875 to 0.21875
- up_bias: float32 [3072], replicated, may hold values from -2 to 2
- down_weight: bfloat16 [3072, 768], replicated, may hold values from -0.109375 to 0.109375
- down_bias: float32 [768], replicated, may hold values from -2 to 2
- cotangent: bfloat16 [65536, 768], P(('seq', 'dp')), may hold values from -6 to 6
- row_counts: int32 [64, 2], P('dp'), may hold values from 128 to 512, as said below
- image_lengths: int32 [64, 4], P('dp'), may hold values from 1 to 1021, as said below
Outputs:
- layer_out: bfloat16 [65536, 768], P(('seq', 'dp'))
- grad_tokens: bfloat16 [65536, 768], P(('seq', 'dp'))
- grad_input_weight: float32 [768, 2304], P('dp')
- grad_query_bias: float32 [768], P('dp')
- grad_value_bias: float32 [768], P('dp')
- grad_out_weight: float32 [768, 768], P('dp')
- grad_out_bias: float32 [768], P('dp')
- grad_first_gain: float32 [768], P('dp')
- grad_first_shift: float32 [768], P('dp')
- grad_second_gain: float32 [768], P('dp')
- grad_second_shift: float32 [768], P('dp')
- grad_up_weight: float32 [768, 3072], P('dp')
- grad_up_bias: float32 [3072], P('dp')
- grad_down_weight: float32 [3072, 768], P('dp')
- grad_down_bias: float32 [768], P('dp')
Inputs may be any that keep to these rules, and one draw needn't show every extreme that they name: row_counts[n, s] is the number of used rows of part s of sequence n; in every sequence one of the two counts is exactly 512. `image_lengths`: the 4 lengths of a sequence sum to its two row counts together; the third image holds the last used row of part 0 and the first row of part 1.
All inputs are finite; a program needn't handle non-finite values.
Results may differ from a plain program's by a relative error of at most 0.015.
Values may be sent and summed in bfloat16 or wider, within the bound.
A program may use at most 256 MiB of HBM per device.

v0:
```python
import jax
import jax.numpy as jnp
from jax import lax
from jax.experimental import pallas as pl
from jax.experimental.pallas import tpu as pltpu
from jax.sharding import PartitionSpec as P

F32 = jnp.float32
BF = jnp.bfloat16
EPS = 1e-06
ROWS = 512
WIDTH = 768
TILE = 256
CHUNKS = 11
SLOTS = 7
FEATURES = 37
PARTS = (
    ((2, 0, 768),),
    ((0, 0, 768),),
    ((1, 0, 768),),
    ((0, 0, 768),),
    ((1, 0, 768),),
    ((0, 0, 768),),
    ((1, 0, 768),),
    ((0, 0, 768),),
    ((1, 0, 768),),
    ((0, 0, 768),),
    ((0, 0, 256), (1, 256, 512), (2, 512, 768)),
)
Y_FIRST = (0, 10)
STEPS = [(c, 0, 0) for c in range(CHUNKS)]
STEPS += [(c, s, p) for c in range(CHUNKS) for p, _, _ in PARTS[c] for s in (1, 2, 3)]
STEPS += [(c, 4, 2) for c in Y_FIRST]
STEPS += [(c, 5, p) for c in range(CHUNKS) for p, _, _ in PARTS[c] if p < 2]
MESH = pl.DeviceIdType.MESH


def dot_nn(left, right):
    return lax.dot_general(left, right, (((1,), (0,)), ((), ())), preferred_element_type=F32)


def dot_nt(left, right):
    return lax.dot_general(left, right, (((1,), (1,)), ((), ())), preferred_element_type=F32)


def dot_tn(left, right):
    return lax.dot_general(left, right, (((0,), (0,)), ((), ())), preferred_element_type=F32)


def norm_parts(block):
    centred = block - jnp.mean(block, axis=-1, keepdims=True)
    spread = jnp.mean(centred * centred, axis=-1, keepdims=True)
    inverse = lax.rsqrt(spread + EPS)
    return centred * inverse, inverse


def kernel(
    counts_ref,
    lengths_ref,
    tokens_hbm,
    cot_hbm,
    wi_hbm,
    wo_hbm,
    wu_hbm,
    wd_hbm,
    qb_ref,
    vb_ref,
    ob_ref,
    fg_ref,
    fs_ref,
    sg_ref,
    ss_ref,
    ub_ref,
    db_ref,
    lo_hbm,
    gt_hbm,
    gi_ref,
    gqb_ref,
    gvb_ref,
    go_ref,
    gob_ref,
    gfg_ref,
    gfs_ref,
    gsg_ref,
    gss_ref,
    gu_ref,
    gub_ref,
    gd_ref,
    gdb_ref,
    W,
    CH,
    R0,
    R1,
    R2,
    R3,
    S1,
    S2,
    S3,
    S4,
    FT,
    FDO,
    STAT,
    FSTAT,
    QO,
    KO,
    VO,
    QF,
    KF,
    VF,
    TOK,
    COT,
    ATT,
    SEC,
    ACT,
    DH,
    XT,
    RES,
    ACC,
    MF,
    PB,
    TOP,
    SUM,
    VS,
    VR,
    wsem,
    iosem,
    xsend,
    xrecv,
    rsend,
    rrecv,
    vsend,
    vrecv,
):
    ACC1, ACC2 = ACC.at[0], ACC.at[1]
    part = lax.axis_index("seq")
    dp = lax.axis_index("dp")
    y_lo = dp // 32
    z = (dp // 8) % 4
    x = (dp // 2) % 4
    core = dp % 2
    y = 2 * part + y_lo

    def device(yy, zz, xx, cc):
        return (yy // 2, ((yy % 2) * 4 + zz) * 8 + xx * 2 + cc)

    sibling = device(y, z, x, 1 - core)
    z_of = [(z + k) % 4 for k in range(4)]
    x_of = [(x + k) % 4 for k in range(4)]
    y_of = [(y + k) % 4 for k in range(4)]
    z_a, z_b = z + 1 - 2 * (z % 2), 3 - z
    x_a, x_b = x + 1 - 2 * (x % 2), 3 - x
    near_z = [device(y, v, x, core) for v in (z_a, z_b)]
    near_x = [device(y, z, v, core) for v in (x_a, x_b)]
    z_peer = [device(y, v, x, core) for v in z_of]
    x_peer = [device(y, z, v, core) for v in x_of]
    y_peer = [device(v, z, x, core) for v in y_of]
    partner = y_peer[2]

    def load(src, dst, sem):
        copy = pltpu.make_async_copy(src, dst, sem)
        copy.start()
        return copy

    tok_load = load(tokens_hbm, TOK, iosem.at[0])
    w_load = {}
    for i in range(3):
        w_load[i] = load(wi_hbm.at[:, pl.ds(WIDTH * i, WIDTH)], W.at[i], wsem.at[i])
    cot_load = load(cot_hbm, COT, iosem.at[1])
    w_load[3] = load(wo_hbm, W.at[3], wsem.at[3])

    def load_ffn(f):
        slot = f % 2
        up = load(wu_hbm.at[:, pl.ds(WIDTH * f, WIDTH)], W.at[4 + slot], wsem.at[4 + slot])
        down = load(wd_hbm.at[pl.ds(WIDTH * f, WIDTH)], W.at[6 + slot], wsem.at[6 + slot])
        return up, down

    ffn_load = {0: load_ffn(0), 1: load_ffn(1)}

    barrier = pltpu.get_barrier_semaphore()
    for peer in [sibling] + z_peer[1:] + x_peer[1:] + y_peer[1:]:
        pl.semaphore_signal(barrier, inc=1, device_id=peer, device_id_type=MESH)
    pl.semaphore_wait(barrier, 10)

    def remote(src, dst, send, recv, peer):
        copy = pltpu.make_async_remote_copy(
            src_ref=src,
            dst_ref=dst,
            send_sem=send,
            recv_sem=recv,
            device_id=peer,
            device_id_type=MESH,
        )
        copy.start()
        return copy

    far_tokens = []
    for r in range(2):
        half = pl.ds(TILE * r, TILE)
        far_tokens.append(
            remote(tokens_hbm.at[half], FT.at[half], xsend.at[r], xrecv.at[r], partner)
        )

    def all_bytes(ref, sem):
        pltpu.make_async_copy(ref, ref, sem).wait()

    landing = {}

    def send_all(key, dst, copies):
        i = STEPS.index(key)
        landing[key] = dst
        for src, into, peer in copies:
            remote(src, into, rsend.at[i], rrecv.at[i], peer)

    def received(key):
        all_bytes(landing[key], rrecv.at[STEPS.index(key)])

    def gone(key):
        all_bytes(landing.pop(key), rsend.at[STEPS.index(key)])

    def rs_core(c):
        src = CH.at[c % SLOTS, :, :, :, 1 - core]
        send_all((c, 0, 0), R0.at[c], [(src, R0.at[c], sibling)])

    def y_slot(c):
        n = Y_FIRST.index(c)
        return n, 384 if n == 0 else 128

    def rs_first(c):
        received((c, 0, 0))

        def add(i, carry):
            yl, zz = i // 4, i % 4
            R0[c, yl, zz] = (
                R0[c, yl, zz].astype(F32) + CH[c % SLOTS, yl, zz, :, core].astype(F32)
            ).astype(BF)
            return carry

        lax.fori_loop(0, 8, add, 0)
        for p, lo, hi in PARTS[c]:
            copies = []
            if p == 2:
                n, width = y_slot(c)
                whole = S1.at[n, :, :, :, :, 0:width]
                for k in (2, 1, 3):
                    start = pl.multiple_of(lo + width * (y_of[k] // 2), 128)
                    src = R0.at[c, y_of[k] % 2, :, :, :, pl.ds(start, width)]
                    copies.append((src, S1.at[n, k - 1, :, :, :, 0:width], y_peer[k]))
            else:
                whole = R1.at[c, 0:2, :, :, :, lo:hi]
                a, b = (z_a, z_b) if p == 0 else (x_a, x_b)
                across = 3 - a
                peers = near_z if p == 0 else near_x
                for half, nearest in ((0, a), (1, b)):
                    for spot, wanted in ((1, across), (0, nearest)):
                        dst = R1.at[c, half, spot, :, :, lo:hi]
                        copies.append((shares(c, p, half, wanted, lo, hi), dst, peers[half]))
            send_all((c, 1, p), whole, copies)

    def shares(c, p, yl, v, lo, hi):
        if p == 0:
            return R0.at[c, yl, v, :, :, lo:hi]
        return R0.at[c, yl, :, v, :, lo:hi]

    def rs_mid(c):
        for p, lo, hi in PARTS[c]:
            if p == 2:
                continue
            received((c, 1, p))
            v, a, b = (z, z_a, z_b) if p == 0 else (x, x_a, x_b)
            for half, other in ((0, b), (1, a)):
                for spot, kept in ((0, v), (1, other)):
                    at = (c, half, spot, slice(None), slice(None), slice(lo, hi))
                    own = shares(c, p, half, kept, lo, hi)[...]
                    R1[at] = (own.astype(F32) + R1[at].astype(F32)).astype(BF)
            peers = near_z if p == 0 else near_x
            copies = []
            for half in range(2):
                src = R1.at[c, half, 1, :, :, lo:hi]
                copies.append((src, R1.at[c, 2, half, :, :, lo:hi], peers[1 - half]))
            send_all((c, 5, p), R1.at[c, 2, :, :, :, lo:hi], copies)

    def rs_second(c):
        for p, lo, hi in PARTS[c]:
            received((c, 1 if p == 2 else 5, p))
            copies = []
            if p == 2:
                n, width = y_slot(c)
                start = pl.multiple_of(lo + width * part, 128)
                for zz in range(4):
                    total = R0[c, y_lo, zz, :, :, pl.ds(start, width)].astype(F32)
                    for k in range(3):
                        total = total + S1[n, k, zz, :, :, 0:width].astype(F32)
                    S1[n, 0, zz, :, :, 0:width] = total.astype(BF)
                whole = S2.at[n, :, :, :, 0:width]
            else:
                for half in range(2):
                    at = (c, half, 0, slice(None), slice(None), slice(lo, hi))
                    total = R1[at].astype(F32) + R1[c, 2, half, :, :, lo:hi].astype(F32)
                    R1[at] = total.astype(BF)
                whole = R2.at[c, :, :, :, lo:hi]
            for k in (2, 1, 3):
                if p == 0:
                    src = R1.at[c, 0:2, 0, x_of[k], :, lo:hi]
                    dst, peer = R2.at[c, k - 1, :, :, lo:hi], x_peer[k]
                elif p == 1:
                    src = R1.at[c, 0:2, 0, z_of[k], :, lo:hi]
                    dst, peer = R2.at[c, k - 1, :, :, lo:hi], z_peer[k]
                else:
                    src = S1.at[n, 0, z_of[k], :, :, 0:width]
                    dst, peer = S2.at[n, k - 1, :, :, 0:width], z_peer[k]
                copies.append((src, dst, peer))
            send_all((c, 2, p), whole, copies)

    def rs_third(c):
        for p, lo, hi in PARTS[c]:
            received((c, 2, p))
            copies = []
            if p == 2:
                n, width = y_slot(c)
                total = S1[n, 0, z, :, :, 0:width].astype(F32)
                for k in range(3):
                    total = total + S2[n, k, :, :, 0:width].astype(F32)
                S2[n, 0, :, :, 0:width] = total.astype(BF)
                whole = S3.at[n, :, :, 0:width]
            else:
                if p == 0:
                    total = R1[c, 0:2, 0, x, :, lo:hi].astype(F32)
                else:
                    total = R1[c, 0:2, 0, z, :, lo:hi].astype(F32)
                for k in range(3):
                    total = total + R2[c, k, :, :, lo:hi].astype(F32)
                R2[c, 0, :, :, lo:hi] = total.astype(BF)
                whole = R3.at[c, :, :, lo:hi]
            for k in (2, 1, 3):
                if p == 2:
                    src = S2.at[n, 0, x_of[k], :, 0:width]
                    dst, peer = S3.at[n, k - 1, :, 0:width], x_peer[k]
                else:
                    src = R2.at[c, 0, y_of[k] % 2, :, lo:hi]
                    dst, peer = R3.at[c, k - 1, :, lo:hi], y_peer[k]
                copies.append((src, dst, peer))
            send_all((c, 3, p), whole, copies)

    def store_share(c, lo, hi, total):
        if c < 4:
            gu_ref[:, WIDTH * c + lo : WIDTH * c + hi] = total[0:12]
        elif c < 7:
            gd_ref[16 * (c - 4) : 16 * (c - 3), lo:hi] = total
        elif c == 7:
            go_ref[:, lo:hi] = total[0:12]
        else:
            for b in range(lo // TILE, hi // TILE):
                start = WIDTH * b + TILE * (c - 8)
                gi_ref[:, start : start + TILE] = total[0:12, TILE * b - lo : TILE * (b + 1) - lo]

    def rs_fourth(c):
        for p, lo, hi in PARTS[c]:
            received((c, 3, p))
            if p == 2:
                n, width = y_slot(c)
                total = S2[n, 0, x, :, 0:width].astype(F32)
                for k in range(3):
                    total = total + S3[n, k, :, 0:width].astype(F32)
                S4[n, 0, :, 0:width] = total
                dst = S4.at[n, 1, :, 0:width]
                send_all((c, 4, p), dst, [(S4.at[n, 0, :, 0:width], dst, partner)])
            else:
                total = (R2[c, 0, y_lo, :, lo:hi].astype(F32) + R3[c, 1, :, lo:hi].astype(F32)) + (
                    R3[c, 0, :, lo:hi].astype(F32) + R3[c, 2, :, lo:hi].astype(F32)
                )
                store_share(c, lo, hi, total)

    def rs_end(c):
        n, width = y_slot(c)
        received((c, 4, 2))
        mine = S4[n, 0, :, 0:width]
        other = S4[n, 1, :, 0:width]
        low = jnp.where(part == 0, mine, other)
        high = jnp.where(part == 0, other, mine)
        lo = PARTS[c][-1][1]
        store_share(c, lo, lo + 2 * width, jnp.concatenate([low, high], axis=1))

    counts0 = counts_ref[0, 0]
    counts1 = counts_ref[0, 1]
    end0 = lengths_ref[0, 0]
    end1 = end0 + lengths_ref[0, 1]
    end2 = end1 + lengths_ref[0, 2]
    end3 = end2 + lengths_ref[0, 3]

    def used_rows(start, size, width):
        place = lax.broadcasted_iota(jnp.int32, (size, width), 0) + start
        return place < counts0 + part * (counts1 - counts0)

    def features(base, which):
        place = lax.broadcasted_iota(jnp.int32, (ROWS, 128), 0)
        shifted = place + which * counts0
        index = jnp.zeros((ROWS, 128), jnp.int32)
        for end in (end0, end1, end2, end3):
            index = index + jnp.where(end <= shifted, 1, 0)
        owned = counts0 + which * (counts1 - counts0)
        ids = jnp.where(place < owned, index, 4 + which * ROWS + place)
        lane = lax.broadcasted_iota(jnp.int32, (ROWS, 128), 1)
        high = lane >= 64
        spot = jnp.where(high, lane - 64, lane)
        digit = jnp.where(
            spot < 16, ids & 15, jnp.where(spot < 32, ((ids >> 4) & 15) + 16, (ids >> 8) + 32)
        )
        hot = jnp.where(digit == spot, 1.0, 0.0)
        query = jnp.where(spot < FEATURES, 1.0 - hot, 0.0)
        key = hot * -1e30
        MF[base] = jnp.where(high, query, 0.0).astype(BF)
        MF[base + 1] = jnp.where(high, 0.0, query).astype(BF)
        MF[base + 2] = jnp.where(high, key, 0.0).astype(BF)
        MF[base + 3] = jnp.where(high, 0.0, key).astype(BF)

    features(0, part)
    features(4, 1 - part)
    lane_row = lax.broadcasted_iota(jnp.int32, (1, 128), 1)
    select = [
        jnp.where(lane_row < 64, 1.0, 0.0).astype(BF),
        jnp.where(lane_row < 64, 0.0, 1.0).astype(BF),
    ]

    rho = lax.broadcasted_iota(jnp.int32, (ROWS, 384), 0)
    feature = lax.broadcasted_iota(jnp.int32, (ROWS, 384), 1)
    within = rho & 15
    PB[...] = jnp.where(
        (within < 12) & (feature == (rho >> 4) * 12 + within), 1.0, 0.0
    ).astype(BF)

    def padded_transpose(source):
        for b in range(2):
            XT[ROWS * b : ROWS * (b + 1), :] = dot_nt(
                PB[...], source[:, 384 * b : 384 * (b + 1)]
            ).astype(BF)

    def chunk_matmul(c, right):
        def block(m, carry):
            start = pl.multiple_of(m * TILE, TILE)
            out = dot_nn(XT[pl.ds(start, TILE), :], right())
            CH[c % SLOTS, m // 2, pl.ds(2 * (m % 2), 2)] = out.astype(BF).reshape(
                2, 4, 2, 16, WIDTH
            )
            return carry

        lax.fori_loop(0, 4, block, 0)

    ones = jnp.ones((16, ROWS), BF)

    def row_sum(block):
        return dot_nn(ones, block)[0:1]

    def tiles(step):
        def run(t, carry):
            step(pl.ds(pl.multiple_of(t * TILE, TILE), TILE), t * TILE)
            return carry

        lax.fori_loop(0, ROWS // TILE, run, 0)

    qb = qb_ref[...].reshape(1, WIDTH)
    vb = vb_ref[...].reshape(1, WIDTH)
    ob = ob_ref[...].reshape(1, WIDTH)
    fg = fg_ref[...].reshape(1, WIDTH)
    fs = fs_ref[...].reshape(1, WIDTH)
    sg = sg_ref[...].reshape(1, WIDTH)
    ss = ss_ref[...].reshape(1, WIDTH)
    db = db_ref[...].reshape(1, WIDTH)

    def projection(source, q_ref, k_ref, v_ref):
        def step(rows, start):
            unit, _ = norm_parts(source[rows, :].astype(F32))
            normed = (unit * fg + fs).astype(BF)
            q = (dot_nn(normed, W[0]) + qb).astype(BF)
            q_ref[rows, :] = q * jnp.asarray(0.125, BF)
            k_ref[rows, :] = dot_nn(normed, W[1]).astype(BF)
            v_ref[rows, :] = (dot_nn(normed, W[2]) + vb).astype(BF)

        return step

    tok_load.wait()
    for i in range(3):
        w_load[i].wait()
    tiles(projection(TOK, QO, KO, VO))

    cot_load.wait()

    def mask_cot(rows, start):
        used = used_rows(start, TILE, WIDTH)
        COT[rows, :] = jnp.where(used, COT[rows, :].astype(F32), 0.0).astype(BF)

    tiles(mask_cot)

    def pair_cols(hp):
        return pl.ds(pl.multiple_of(hp * 128, 128), 128)

    def mix_at(hp, h):
        start = pl.multiple_of(128 * (hp % 4) + 64 * h, 64)
        return hp // 4, pl.ds(start, 64), slice(0, ROWS)

    def attend_own(hp, carry):
        cols = pair_cols(hp)
        q = QO[:, cols]
        keys = KO[:, cols]
        values = VO[:, cols].T
        for h in range(2):
            row = pl.ds(2 * hp + h, 1)
            scores = dot_nt(keys * select[h] + MF[2 + h], q * select[h] + MF[h])
            top = jnp.max(scores, axis=0, keepdims=True)
            probs = jnp.exp(scores - top)
            TOP[row, :] = top
            SUM[row, :] = jnp.sum(probs, axis=0, keepdims=True)
            own = slice(64 * h, 64 * h + 64)
            ACC[mix_at(hp, h)] = dot_nn(values[own], probs.astype(BF))
        return carry

    lax.fori_loop(0, 6, attend_own, 0)

    def attend_far(r):
        rows = slice(TILE * r, TILE * (r + 1))

        def step(hp, carry):
            cols = pair_cols(hp)
            q = QO[:, cols]
            keys = KF[rows, cols]
            values = VF[rows, cols].T
            outs = []
            for h in range(2):
                row = pl.ds(2 * hp + h, 1)
                own = slice(64 * h, 64 * h + 64)
                scores = dot_nt(keys * select[h] + MF[6 + h, rows], q * select[h] + MF[h])
                before = TOP[row, :]
                top = jnp.maximum(before, jnp.max(scores, axis=0, keepdims=True))
                shrink = jnp.exp(before - top)
                probs = jnp.exp(scores - top)
                total = SUM[row, :] * shrink + jnp.sum(probs, axis=0, keepdims=True)
                mixed = ACC[mix_at(hp, h)] * shrink + dot_nn(values[own], probs.astype(BF))
                if r == 0:
                    TOP[row, :] = top
                    SUM[row, :] = total
                    ACC[mix_at(hp, h)] = mixed
                else:
                    STAT[0, row, :] = top + jnp.log(total)
                    outs.append(mixed * (1.0 / total))
            if r == 1:
                ATT[:, cols] = jnp.concatenate(outs, axis=0).T.astype(BF)
            return carry

        return step

    for r in range(2):
        far_tokens[r].wait_recv()
        projection(FT, QF, KF, VF)(pl.ds(TILE * r, TILE), TILE * r)
        lax.fori_loop(0, 6, attend_far(r), 0)

    w_load[3].wait()

    def out_step(rows, start):
        res = TOK[rows, :].astype(F32) + dot_nn(ATT[rows, :], W[3]) + ob
        RES[rows, :] = res
        unit, _ = norm_parts(res)
        SEC[rows, :] = (unit * sg + ss).astype(BF)
        ACC1[rows, :] = jnp.zeros((TILE, WIDTH), F32)
        ACC2[rows, :] = jnp.zeros((TILE, WIDTH), F32)

    tiles(out_step)
    padded_transpose(SEC)
    VS[0] = jnp.zeros((16, WIDTH), F32)

    for f in range(4):
        slot = f % 2
        for copy in ffn_load[f]:
            copy.wait()
        ub = ub_ref[WIDTH * f : WIDTH * (f + 1)].reshape(1, WIDTH)

        def ffn_step(rows, start, slot=slot, ub=ub):
            dout = COT[rows, :]
            hidden = dot_nn(SEC[rows, :], W[4 + slot]) + ub
            cdf = 0.5 * (1.0 + lax.erf(hidden * 0.7071067811865476))
            density = jnp.exp(-0.5 * hidden * hidden) * 0.3989422804014327
            active = (hidden * cdf).astype(BF)
            ACT[rows, :] = active
            dhidden = (dot_nt(dout, W[6 + slot]) * (cdf + hidden * density)).astype(BF)
            DH[rows, :] = dhidden
            ACC1[rows, :] += dot_nn(active, W[6 + slot])
            ACC2[rows, :] += dot_nt(dhidden, W[4 + slot])

        tiles(ffn_step)
        if f + 2 < 4:
            ffn_load[f + 2] = load_ffn(f + 2)
        chunk_matmul(f, lambda: DH[...])
        rs_core(f)
        VS[0, 8 + f : 9 + f, :] = row_sum(DH[...])

        def down_step(b, carry, f=f):
            cols = pl.ds(pl.multiple_of(b * 384, 384), 384)
            out = dot_tn(ACT[:, cols], COT[...]).astype(BF).reshape(4, 2, 3, 16, WIDTH)
            for k in range(3):
                CH[4 + k, f // 2, 2 * (f % 2) + b] = out[:, :, k]
            return carry

        lax.fori_loop(0, 2, down_step, 0)
        if f >= 1:
            rs_first(f - 1)

    rs_mid(1)
    for k in range(3):
        rs_core(4 + k)

    def second_back(rows, start):
        res = RES[rows, :]
        used = used_rows(start, TILE, WIDTH)
        FT[rows, :] = jnp.where(used, res + ACC1[rows, :] + db, 0.0).astype(BF)
        unit, inverse = norm_parts(res)
        dsecond = ACC2[rows, :]
        VS[0, 5:6, :] += jnp.sum(dsecond * unit, axis=0, keepdims=True)
        VS[0, 6:7, :] += jnp.sum(dsecond, axis=0, keepdims=True)
        g = dsecond * sg
        through = (
            g
            - jnp.mean(g, axis=-1, keepdims=True)
            - unit * jnp.mean(g * unit, axis=-1, keepdims=True)
        ) * inverse
        dres = COT[rows, :].astype(F32) + through
        RES[rows, :] = dres
        SEC[rows, :] = dres.astype(BF)
        DH[rows, :] = dot_nt(dres.astype(BF), W[3]).astype(BF)

    tiles(second_back)
    lo_store = load(FT, lo_hbm, iosem.at[2])
    far_dout = []
    for r in range(2):
        half = pl.ds(384 * r, 384)
        far_dout.append(
            remote(DH.at[:, half], FDO.at[:, half], xsend.at[2 + r], xrecv.at[2 + r], partner)
        )
    rs_first(3)
    rs_second(0)
    VS[0, 7:8, :] = row_sum(COT[...])
    VS[0, 2:3, :] = row_sum(SEC[...])

    head = lax.broadcasted_iota(jnp.int32, (16, WIDTH), 0)
    column = lax.broadcasted_iota(jnp.int32, (16, WIDTH), 1)
    in_head = jnp.where((column >> 6) == head, 1.0, 0.0).astype(BF)
    product = DH[...].astype(F32) * ATT[...].astype(F32)
    rough = product.astype(BF)
    STAT[1] = dot_nt(in_head, rough) + dot_nt(in_head, (product - rough.astype(F32)).astype(BF))
    far_stats = remote(STAT, FSTAT, xsend.at[4], xrecv.at[4], partner)

    padded_transpose(ATT)
    gone((0, 0, 0))
    chunk_matmul(7, lambda: SEC[...])
    rs_core(7)
    rs_first(4)
    rs_mid(2)
    rs_second(1)
    rs_first(5)

    def own_queries(hp, carry):
        cols = pair_cols(hp)
        q = QO[:, cols]
        ko = KO[:, cols]
        kf = KF[:, cols]
        vo = VO[:, cols]
        vf = VF[:, cols]
        do = DH[:, cols]
        ko_t = ko.T
        kf_t = kf.T
        dq = []
        dk = None
        for h in range(2):
            logsum = STAT[0, pl.ds(2 * hp + h, 1), :]
            delta = STAT[1, pl.ds(2 * hp + h, 1), :]
            qm = q * select[h] + MF[h]
            qs = q * select[h]
            dom = do * select[h]
            near = jnp.exp(dot_nt(ko * select[h] + MF[2 + h], qm) - logsum)
            dnear = (near * (dot_nt(vo, dom) - delta)).astype(BF)
            far = jnp.exp(dot_nt(kf * select[h] + MF[6 + h], qm) - logsum)
            dfar = (far * (dot_nt(vf, dom) - delta)).astype(BF)
            dq.append(
                dot_nn(ko_t[64 * h : 64 * h + 64], dnear)
                + dot_nn(kf_t[64 * h : 64 * h + 64], dfar)
            )
            dk_h = dot_nn(dnear, qs)
            dv_h = dot_nn(near.astype(BF), dom)
            dk, dv = (dk_h, dv_h) if dk is None else (dk + dk_h, dv + dv_h)
        ACC1[:, cols] = dk
        ACC2[:, cols] = dv
        QO[:, cols] = (jnp.concatenate(dq, axis=0).T * 0.125).astype(BF)
        return carry

    lax.fori_loop(0, 2, own_queries, 0)
    rs_mid(3)
    rs_first(6)
    lax.fori_loop(2, 4, own_queries, 0)
    rs_first(7)
    rs_mid(4)
    rs_mid(5)
    rs_second(2)
    rs_third(0)
    rs_third(1)
    lax.fori_loop(4, 6, own_queries, 0)
    rs_mid(6)
    rs_second(3)
    rs_second(4)
    rs_third(2)

    def again(rows, start):
        unit, _ = norm_parts(TOK[rows, :].astype(F32))
        ATT[rows, :] = (unit * fg + fs).astype(BF)

    tiles(again)
    padded_transpose(ATT)

    far_stats.wait_recv()

    def far_queries(hp, carry):
        cols = pair_cols(hp)
        q = QF[:, cols]
        ko = KO[:, cols]
        vo = VO[:, cols]
        do = FDO[:, cols]
        dk = ACC1[:, cols]
        dv = ACC2[:, cols]
        for h in range(2):
            logsum = FSTAT[0, pl.ds(2 * hp + h, 1), :]
            delta = FSTAT[1, pl.ds(2 * hp + h, 1), :]
            qs = q * select[h]
            dom = do * select[h]
            probs = jnp.exp(dot_nt(ko * select[h] + MF[2 + h], qs + MF[4 + h]) - logsum)
            dscores = (probs * (dot_nt(vo, dom) - delta)).astype(BF)
            dk = dk + dot_nn(dscores, qs)
            dv = dv + dot_nn(probs.astype(BF), dom)
        KO[:, cols] = dk.astype(BF)
        VO[:, cols] = dv.astype(BF)
        return carry

    for j in range(3):
        c = 8 + j
        if j < 2:
            far_dout[j].wait_recv()
        lax.fori_loop(2 * j, 2 * j + 2, far_queries, 0)
        gone((c - 7, 0, 0))
        cols = slice(TILE * j, TILE * (j + 1))

        def joined(cols=cols):
            return jnp.concatenate([QO[:, cols], KO[:, cols], VO[:, cols]], axis=1)

        chunk_matmul(c, joined)
        rs_core(c)
        if j == 0:
            rs_mid(7)
            rs_second(5)
            rs_second(6)
            rs_third(3)
            rs_third(4)
            rs_fourth(0)
            rs_fourth(1)
        if j == 1:
            rs_first(8)
            rs_second(7)
            rs_third(5)
            rs_third(6)
            rs_fourth(2)
            rs_fourth(3)
            rs_end(0)
        if j == 2:
            rs_first(9)
            rs_mid(8)
            rs_third(7)
            rs_fourth(4)
            rs_fourth(5)

    VS[0, 0:1, :] = row_sum(QO[...])
    VS[0, 1:2, :] = row_sum(VO[...])

    def first_back(rows, start):
        unit, inverse = norm_parts(TOK[rows, :].astype(F32))
        dnormed = (
            dot_nt(QO[rows, :], W[0]) + dot_nt(KO[rows, :], W[1]) + dot_nt(VO[rows, :], W[2])
        )
        VS[0, 3:4, :] += jnp.sum(dnormed * unit, axis=0, keepdims=True)
        VS[0, 4:5, :] += jnp.sum(dnormed, axis=0, keepdims=True)
        g = dnormed * fg
        through = (
            g
            - jnp.mean(g, axis=-1, keepdims=True)
            - unit * jnp.mean(g * unit, axis=-1, keepdims=True)
        ) * inverse
        TOK[rows, :] = (RES[rows, :] + through).astype(BF)

    for copy in far_tokens:
        copy.wait_send()
    tiles(first_back)
    gt_store = load(TOK, gt_hbm, iosem.at[3])

    def vec_send(step, peers):
        base = (0, 1, 4, 7)[step]
        for i, peer in enumerate(peers):
            remote(VS.at[step], VR.at[base + i], vsend.at[step], vrecv.at[step], peer)

    def vec_add(step):
        base = (0, 1, 4, 7)[step]
        if step == 0:
            all_bytes(VR.at[0:1], vrecv.at[0])
            total = VS[0] + VR[0]
        else:
            all_bytes(VR.at[base : base + 3], vrecv.at[step])
            total = (VS[step] + VR[base + 1]) + (VR[base] + VR[base + 2])
        VS[step + 1] = total

    vec_send(0, [sibling])
    rs_first(10)
    rs_mid(9)
    rs_second(8)
    rs_fourth(6)
    rs_fourth(7)
    vec_add(0)
    vec_send(1, z_peer[1:])
    rs_mid(10)
    rs_second(9)
    rs_third(8)
    vec_add(1)
    vec_send(2, x_peer[1:])
    rs_second(10)
    rs_third(9)
    rs_fourth(8)
    vec_add(2)
    vec_send(3, y_peer[1:])
    rs_third(10)
    rs_fourth(9)
    rs_fourth(10)
    vec_add(3)
    rs_end(10)

    spot = lax.broadcasted_iota(jnp.int32, (WIDTH, 128), 0)
    lane = lax.broadcasted_iota(jnp.int32, (WIDTH, 128), 1)
    narrow = jnp.where((lane < 12) & (spot == lane + 12 * dp), 1.0, 0.0)
    wide = jnp.where((lane < 48) & (spot == lane + 48 * (dp % 16)), 1.0, 0.0)
    vectors = VS[4]
    exact = dict(precision=lax.Precision.HIGHEST, preferred_element_type=F32)
    small = jnp.dot(vectors, narrow, **exact)
    large = jnp.dot(vectors, wide, **exact)
    row = lax.broadcasted_iota(jnp.int32, (16, 128), 0)
    large = jnp.sum(jnp.where(row == 8 + dp // 16, large, 0.0), axis=0, keepdims=True)
    for i, ref in enumerate(
        (gqb_ref, gvb_ref, gob_ref, gfg_ref, gfs_ref, gsg_ref, gss_ref, gdb_ref)
    ):
        ref[...] = small[i : i + 1, 0:12].reshape(12)
    gub_ref[...] = large[:, 0:48].reshape(48)

    for copy in far_dout:
        copy.wait_send()
    far_stats.wait_send()
    for key in list(landing):
        gone(key)
    all_bytes(VR.at[0:1], vsend.at[0])
    for step in range(1, 4):
        all_bytes(VR.at[3 * step - 2 : 3 * step + 1], vsend.at[step])
    lo_store.wait()
    gt_store.wait()


def finish(*refs):
    count = len(refs) // 2
    for i in range(count):
        refs[count + i][...] = refs[i][...]


def body(
    tokens,
    input_weight,
    query_bias,
    value_bias,
    out_weight,
    out_bias,
    first_gain,
    first_shift,
    second_gain,
    second_shift,
    up_weight,
    up_bias,
    down_weight,
    down_bias,
    cotangent,
    row_counts,
    image_lengths,
):
    hbm = pl.BlockSpec(memory_space=pl.ANY)
    vmem = pl.BlockSpec(memory_space=pltpu.VMEM)
    smem = pl.BlockSpec(memory_space=pltpu.SMEM)
    rows = jax.ShapeDtypeStruct((ROWS, WIDTH), BF)

    def f32(*shape):
        return jax.ShapeDtypeStruct(shape, F32)

    def block(kind, *lead):
        return pltpu.VMEM((*lead, ROWS, WIDTH), kind)

    out = pl.pallas_call(
        kernel,
        out_shape=(
            rows,
            rows,
            f32(12, 3 * WIDTH),
            f32(12),
            f32(12),
            f32(12, WIDTH),
            f32(12),
            f32(12),
            f32(12),
            f32(12),
            f32(12),
            f32(12, 4 * WIDTH),
            f32(48),
            f32(48, WIDTH),
            f32(12),
        ),
        in_specs=[smem, smem] + [hbm] * 6 + [vmem] * 9,
        out_specs=(hbm, hbm) + (vmem,) * 13,
        scratch_shapes=[
            pltpu.VMEM((8, WIDTH, WIDTH), BF),
            pltpu.VMEM((SLOTS, 2, 4, 4, 2, 16, WIDTH), BF),
            pltpu.VMEM((CHUNKS, 2, 4, 4, 16, WIDTH), BF),
            pltpu.VMEM((CHUNKS, 3, 2, 4, 16, WIDTH), BF),
            pltpu.VMEM((CHUNKS, 3, 2, 16, WIDTH), BF),
            pltpu.VMEM((CHUNKS, 3, 16, WIDTH), BF),
            pltpu.VMEM((2, 3, 4, 4, 16, 384), BF),
            pltpu.VMEM((2, 3, 4, 16, 384), BF),
            pltpu.VMEM((2, 3, 16, 384), BF),
            pltpu.VMEM((2, 2, 16, 384), F32),
            block(BF),
            block(BF),
            pltpu.VMEM((2, 16, ROWS), F32),
            pltpu.VMEM((2, 16, ROWS), F32),
        ]
        + [block(BF)] * 12
        + [
            pltpu.VMEM((1024, ROWS), BF),
            block(F32),
            block(F32, 2),
            pltpu.VMEM((8, ROWS, 128), BF),
            pltpu.VMEM((ROWS, 384), BF),
            pltpu.VMEM((16, ROWS), F32),
            pltpu.VMEM((16, ROWS), F32),
            pltpu.VMEM((5, 16, WIDTH), F32),
            pltpu.VMEM((10, 16, WIDTH), F32),
            pltpu.SemaphoreType.DMA((8,)),
            pltpu.SemaphoreType.DMA((4,)),
            pltpu.SemaphoreType.DMA((5,)),
            pltpu.SemaphoreType.DMA((5,)),
            pltpu.SemaphoreType.DMA((len(STEPS),)),
            pltpu.SemaphoreType.DMA((len(STEPS),)),
            pltpu.SemaphoreType.DMA((4,)),
            pltpu.SemaphoreType.DMA((4,)),
        ],
        compiler_params=pltpu.CompilerParams(
            collective_id=0, has_side_effects=True, vmem_limit_bytes=63 * 2**20
        ),
        name="encoder",
    )(
        row_counts,
        image_lengths,
        tokens,
        cotangent,
        input_weight,
        out_weight,
        up_weight,
        down_weight,
        query_bias,
        value_bias,
        out_bias,
        first_gain,
        first_shift,
        second_gain,
        second_shift,
        up_bias,
        down_bias,
    )
    return pl.pallas_call(
        finish,
        out_shape=tuple(jax.ShapeDtypeStruct(value.shape, value.dtype) for value in out),
        in_specs=[vmem] * len(out),
        out_specs=(vmem,) * len(out),
        name="finish",
    )(*out)


def solution(mesh):
    rows = P(("seq", "dp"), None)
    split = P("dp", None)
    line = P("dp")
    return jax.shard_map(
        body,
        mesh=mesh,
        in_specs=(rows,) + (P(),) * 13 + (rows, split, split),
        out_specs=(
            rows,
            rows,
            split,
            line,
            line,
            split,
            line,
            line,
            line,
            line,
            line,
            split,
            line,
            split,
            line,
        ),
        check_vma=False,
    )
```

profile of v0, /device:TPU:0, one launch (start us, length us, event | category | flops | bytes accessed | tf_op | source)
XLA Modules:
  0.0 136.3 jit_solution(2963141980753622745)
XLA Ops:
  0.7 132.5 %encoder.1 = (bf16[512,768]{1,0:T(8,128)(2,1)}, bf16[512,768]{1,0:T(8,128)(2,1)}, f32[12,2304]{1,0:T(8,128)}, f32[12]{0:T(128)}, f32[12]{0:T(128)}, /*index=5*/f...) custom-call(s32[1,2]{1,0:T(1,128)} %counts_ref.1, ...), custom_call_target="tpu_custom_call" | custom-call | tf_op jit(solution)/shard_map/encoder/pallas_call | solution.py:900
  133.2 3.0 %finish.1 = (bf16[512,768]{1,0:T(8,128)(2,1)}, bf16[512,768]{1,0:T(8,128)(2,1)}, f32[12,2304]{1,0:T(8,128)}, f32[12]{0:T(128)}, f32[12]{0:T(128)}, /*index=5*/f3...) custom-call(bf16[512,768]{1,0:T(8,128)(2,1)} %get-tuple-element.30.r, ...), custom_call_target="tpu_custom_call" | custom-call | tf_op jit(solution)/shard_map/finish/pallas_call | solution.py:980
where the time goes:
time: 136 us
  Pallas kernels  135 us (99%)
    pallas_call x1, Pallas kernels, body(): pl.pallas_call(kernel, out_shape=(rows, rows, f32(12, 3 * WIDTH), f32(12)...  132 us
    pallas_call x1, Pallas kernels, body(): pl.pallas_call(finish, out_shape=tuple((jax.ShapeDtypeStruct(value.shape,...  2.96 us

commit v1 on v0

--- a/solution.py
+++ b/solution.py
@@ -24,10 +24,10 @@
     ((1, 0, 768),),
     ((0, 0, 768),),
     ((1, 0, 768),),
-    ((0, 0, 768),),
-    ((0, 0, 256), (1, 256, 512), (2, 512, 768)),
+    ((0, 0, 384), (1, 384, 768)),
+    ((3, 0, 384), (4, 384, 768)),
 )
-Y_FIRST = (0, 10)
+Y_FIRST = (0,)
 STEPS = [(c, 0, 0) for c in range(CHUNKS)]
 STEPS += [(c, s, p) for c in range(CHUNKS) for p, _, _ in PARTS[c] for s in (1, 2, 3)]
 STEPS += [(c, 4, 2) for c in Y_FIRST]
@@ -114,6 +114,7 @@
     ACT,
     DH,
     XT,
+    XN,
     RES,
     ACC,
     MF,
@@ -123,6 +124,7 @@
     VS,
     VR,
     wsem,
+    dsem,
     iosem,
     xsend,
     xrecv,
@@ -175,6 +177,10 @@
         return up, down
 
     ffn_load = {0: load_ffn(0), 1: load_ffn(1)}
+    down_load = [
+        load(wd_hbm.at[pl.ds(2 * WIDTH + ROWS * i, ROWS)], ref, dsem.at[i])
+        for i, ref in enumerate((SEC, ACT, DH))
+    ]
 
     barrier = pltpu.get_barrier_semaphore()
     for peer in [sibling] + z_peer[1:] + x_peer[1:] + y_peer[1:]:
@@ -193,12 +199,7 @@
         copy.start()
         return copy
 
-    far_tokens = []
-    for r in range(2):
-        half = pl.ds(TILE * r, TILE)
-        far_tokens.append(
-            remote(tokens_hbm.at[half], FT.at[half], xsend.at[r], xrecv.at[r], partner)
-        )
+    far_tokens = remote(tokens_hbm, FT, xsend.at[0], xrecv.at[0], partner)
 
     def all_bytes(ref, sem):
         pltpu.make_async_copy(ref, ref, sem).wait()
@@ -221,9 +222,12 @@
         src = CH.at[c % SLOTS, :, :, :, 1 - core]
         send_all((c, 0, 0), R0.at[c], [(src, R0.at[c], sibling)])
 
+    def row_of(c):
+        return c - sum(first < c for first in Y_FIRST)
+
     def y_slot(c):
         n = Y_FIRST.index(c)
-        return n, 384 if n == 0 else 128
+        return n, 384
 
     def rs_first(c):
         received((c, 0, 0))
@@ -245,14 +249,22 @@
                     start = pl.multiple_of(lo + width * (y_of[k] // 2), 128)
                     src = R0.at[c, y_of[k] % 2, :, :, :, pl.ds(start, width)]
                     copies.append((src, S1.at[n, k - 1, :, :, :, 0:width], y_peer[k]))
+            elif p > 2:
+                whole = R1.at[row_of(c), :, :, :, :, lo:hi]
+                for k in (2, 1, 3):
+                    if p == 3:
+                        src, peer = R0.at[c, :, z_of[k], :, :, lo:hi], z_peer[k]
+                    else:
+                        src, peer = R0.at[c, :, :, x_of[k], :, lo:hi], x_peer[k]
+                    copies.append((src, R1.at[row_of(c), k - 1, :, :, :, lo:hi], peer))
             else:
-                whole = R1.at[c, 0:2, :, :, :, lo:hi]
+                whole = R1.at[row_of(c), 0:2, :, :, :, lo:hi]
                 a, b = (z_a, z_b) if p == 0 else (x_a, x_b)
                 across = 3 - a
                 peers = near_z if p == 0 else near_x
                 for half, nearest in ((0, a), (1, b)):
                     for spot, wanted in ((1, across), (0, nearest)):
-                        dst = R1.at[c, half, spot, :, :, lo:hi]
+                        dst = R1.at[row_of(c), half, spot, :, :, lo:hi]
                         copies.append((shares(c, p, half, wanted, lo, hi), dst, peers[half]))
             send_all((c, 1, p), whole, copies)
 
@@ -263,25 +275,25 @@
 
     def rs_mid(c):
         for p, lo, hi in PARTS[c]:
-            if p == 2:
+            if p > 1:
                 continue
             received((c, 1, p))
             v, a, b = (z, z_a, z_b) if p == 0 else (x, x_a, x_b)
             for half, other in ((0, b), (1, a)):
                 for spot, kept in ((0, v), (1, other)):
-                    at = (c, half, spot, slice(None), slice(None), slice(lo, hi))
+                    at = (row_of(c), half, spot, slice(None), slice(None), slice(lo, hi))
                     own = shares(c, p, half, kept, lo, hi)[...]
                     R1[at] = (own.astype(F32) + R1[at].astype(F32)).astype(BF)
             peers = near_z if p == 0 else near_x
             copies = []
             for half in range(2):
-                src = R1.at[c, half, 1, :, :, lo:hi]
-                copies.append((src, R1.at[c, 2, half, :, :, lo:hi], peers[1 - half]))
-            send_all((c, 5, p), R1.at[c, 2, :, :, :, lo:hi], copies)
+                src = R1.at[row_of(c), half, 1, :, :, lo:hi]
+                copies.append((src, R1.at[row_of(c), 2, half, :, :, lo:hi], peers[1 - half]))
+            send_all((c, 5, p), R1.at[row_of(c), 2, :, :, :, lo:hi], copies)
 
     def rs_second(c):
         for p, lo, hi in PARTS[c]:
-            received((c, 1 if p == 2 else 5, p))
+            received((c, 5 if p < 2 else 1, p))
             copies = []
             if p == 2:
                 n, width = y_slot(c)
@@ -292,19 +304,35 @@
                         total = total + S1[n, k, zz, :, :, 0:width].astype(F32)
                     S1[n, 0, zz, :, :, 0:width] = total.astype(BF)
                 whole = S2.at[n, :, :, :, 0:width]
+            elif p > 2:
+                for yl in range(2):
+                    if p == 3:
+                        total = R0[c, yl, z, :, :, lo:hi].astype(F32)
+                    else:
+                        total = R0[c, yl, :, x, :, lo:hi].astype(F32)
+                    for k in range(3):
+                        total = total + R1[row_of(c), k, yl, :, :, lo:hi].astype(F32)
+                    R1[row_of(c), 0, yl, :, :, lo:hi] = total.astype(BF)
+                whole = R2.at[row_of(c), :, :, :, lo:hi]
             else:
                 for half in range(2):
-                    at = (c, half, 0, slice(None), slice(None), slice(lo, hi))
-                    total = R1[at].astype(F32) + R1[c, 2, half, :, :, lo:hi].astype(F32)
+                    at = (row_of(c), half, 0, slice(None), slice(None), slice(lo, hi))
+                    total = R1[at].astype(F32) + R1[row_of(c), 2, half, :, :, lo:hi].astype(F32)
                     R1[at] = total.astype(BF)
-                whole = R2.at[c, :, :, :, lo:hi]
+                whole = R2.at[row_of(c), :, :, :, lo:hi]
             for k in (2, 1, 3):
-                if p == 0:
-                    src = R1.at[c, 0:2, 0, x_of[k], :, lo:hi]
-                    dst, peer = R2.at[c, k - 1, :, :, lo:hi], x_peer[k]
+                if p == 3:
+                    src = R1.at[row_of(c), 0, :, x_of[k], :, lo:hi]
+                    dst, peer = R2.at[row_of(c), k - 1, :, :, lo:hi], x_peer[k]
+                elif p == 4:
+                    src = R1.at[row_of(c), 0, :, z_of[k], :, lo:hi]
+                    dst, peer = R2.at[row_of(c), k - 1, :, :, lo:hi], z_peer[k]
+                elif p == 0:
+                    src = R1.at[row_of(c), 0:2, 0, x_of[k], :, lo:hi]
+                    dst, peer = R2.at[row_of(c), k - 1, :, :, lo:hi], x_peer[k]
                 elif p == 1:
-                    src = R1.at[c, 0:2, 0, z_of[k], :, lo:hi]
-                    dst, peer = R2.at[c, k - 1, :, :, lo:hi], z_peer[k]
+                    src = R1.at[row_of(c), 0:2, 0, z_of[k], :, lo:hi]
+                    dst, peer = R2.at[row_of(c), k - 1, :, :, lo:hi], z_peer[k]
                 else:
                     src = S1.at[n, 0, z_of[k], :, :, 0:width]
                     dst, peer = S2.at[n, k - 1, :, :, 0:width], z_peer[k]
@@ -323,21 +351,25 @@
                 S2[n, 0, :, :, 0:width] = total.astype(BF)
                 whole = S3.at[n, :, :, 0:width]
             else:
-                if p == 0:
-                    total = R1[c, 0:2, 0, x, :, lo:hi].astype(F32)
+                if p == 3:
+                    total = R1[row_of(c), 0, :, x, :, lo:hi].astype(F32)
+                elif p == 4:
+                    total = R1[row_of(c), 0, :, z, :, lo:hi].astype(F32)
+                elif p == 0:
+                    total = R1[row_of(c), 0:2, 0, x, :, lo:hi].astype(F32)
                 else:
-                    total = R1[c, 0:2, 0, z, :, lo:hi].astype(F32)
+                    total = R1[row_of(c), 0:2, 0, z, :, lo:hi].astype(F32)
                 for k in range(3):
-                    total = total + R2[c, k, :, :, lo:hi].astype(F32)
-                R2[c, 0, :, :, lo:hi] = total.astype(BF)
-                whole = R3.at[c, :, :, lo:hi]
+                    total = total + R2[row_of(c), k, :, :, lo:hi].astype(F32)
+                R2[row_of(c), 0, :, :, lo:hi] = total.astype(BF)
+                whole = R3.at[row_of(c), :, :, lo:hi]
             for k in (2, 1, 3):
                 if p == 2:
                     src = S2.at[n, 0, x_of[k], :, 0:width]
                     dst, peer = S3.at[n, k - 1, :, 0:width], x_peer[k]
                 else:
-                    src = R2.at[c, 0, y_of[k] % 2, :, lo:hi]
-                    dst, peer = R3.at[c, k - 1, :, lo:hi], y_peer[k]
+                    src = R2.at[row_of(c), 0, y_of[k] % 2, :, lo:hi]
+                    dst, peer = R3.at[row_of(c), k - 1, :, lo:hi], y_peer[k]
                 copies.append((src, dst, peer))
             send_all((c, 3, p), whole, copies)
 
@@ -349,9 +381,9 @@
         elif c == 7:
             go_ref[:, lo:hi] = total[0:12]
         else:
-            for b in range(lo // TILE, hi // TILE):
-                start = WIDTH * b + TILE * (c - 8)
-                gi_ref[:, start : start + TILE] = total[0:12, TILE * b - lo : TILE * (b + 1) - lo]
+            for b in range(lo // 384, hi // 384):
+                start = 384 * b if c == 8 else WIDTH * (b + 1) + 384 * (c - 9)
+                gi_ref[:, start : start + 384] = total[0:12, 384 * b - lo : 384 * (b + 1) - lo]
 
     def rs_fourth(c):
         for p, lo, hi in PARTS[c]:
@@ -365,8 +397,8 @@
                 dst = S4.at[n, 1, :, 0:width]
                 send_all((c, 4, p), dst, [(S4.at[n, 0, :, 0:width], dst, partner)])
             else:
-                total = (R2[c, 0, y_lo, :, lo:hi].astype(F32) + R3[c, 1, :, lo:hi].astype(F32)) + (
-                    R3[c, 0, :, lo:hi].astype(F32) + R3[c, 2, :, lo:hi].astype(F32)
+                total = (R2[row_of(c), 0, y_lo, :, lo:hi].astype(F32) + R3[row_of(c), 1, :, lo:hi].astype(F32)) + (
+                    R3[row_of(c), 0, :, lo:hi].astype(F32) + R3[row_of(c), 2, :, lo:hi].astype(F32)
                 )
                 store_share(c, lo, hi, total)
 
@@ -428,16 +460,16 @@
         (within < 12) & (feature == (rho >> 4) * 12 + within), 1.0, 0.0
     ).astype(BF)
 
-    def padded_transpose(source):
+    def padded_transpose(source, into):
         for b in range(2):
-            XT[ROWS * b : ROWS * (b + 1), :] = dot_nt(
+            into[ROWS * b : ROWS * (b + 1), :] = dot_nt(
                 PB[...], source[:, 384 * b : 384 * (b + 1)]
             ).astype(BF)
 
     def chunk_matmul(c, right):
         def block(m, carry):
             start = pl.multiple_of(m * TILE, TILE)
-            out = dot_nn(XT[pl.ds(start, TILE), :], right())
+            out = dot_nn((XT if c < 8 else XN)[pl.ds(start, TILE), :], right())
             CH[c % SLOTS, m // 2, pl.ds(2 * (m % 2), 2)] = out.astype(BF).reshape(
                 2, 4, 2, 16, WIDTH
             )
@@ -515,42 +547,61 @@
 
     lax.fori_loop(0, 6, attend_own, 0)
 
-    def attend_far(r):
-        rows = slice(TILE * r, TILE * (r + 1))
-
-        def step(hp, carry):
-            cols = pair_cols(hp)
-            q = QO[:, cols]
-            keys = KF[rows, cols]
-            values = VF[rows, cols].T
-            outs = []
-            for h in range(2):
-                row = pl.ds(2 * hp + h, 1)
-                own = slice(64 * h, 64 * h + 64)
-                scores = dot_nt(keys * select[h] + MF[6 + h, rows], q * select[h] + MF[h])
-                before = TOP[row, :]
-                top = jnp.maximum(before, jnp.max(scores, axis=0, keepdims=True))
-                shrink = jnp.exp(before - top)
-                probs = jnp.exp(scores - top)
-                total = SUM[row, :] * shrink + jnp.sum(probs, axis=0, keepdims=True)
-                mixed = ACC[mix_at(hp, h)] * shrink + dot_nn(values[own], probs.astype(BF))
-                if r == 0:
-                    TOP[row, :] = top
-                    SUM[row, :] = total
-                    ACC[mix_at(hp, h)] = mixed
-                else:
-                    STAT[0, row, :] = top + jnp.log(total)
-                    outs.append(mixed * (1.0 / total))
-            if r == 1:
-                ATT[:, cols] = jnp.concatenate(outs, axis=0).T.astype(BF)
-            return carry
-
-        return step
-
-    for r in range(2):
-        far_tokens[r].wait_recv()
-        projection(FT, QF, KF, VF)(pl.ds(TILE * r, TILE), TILE * r)
-        lax.fori_loop(0, 6, attend_far(r), 0)
+    def attend_far(hp, carry):
+        cols = pair_cols(hp)
+        q = QO[:, cols]
+        keys = KF[:, cols]
+        values = VF[:, cols].T
+        outs = []
+        for h in range(2):
+            row = pl.ds(2 * hp + h, 1)
+            own = slice(64 * h, 64 * h + 64)
+            scores = dot_nt(keys * select[h] + MF[6 + h], q * select[h] + MF[h])
+            before = TOP[row, :]
+            top = jnp.maximum(before, jnp.max(scores, axis=0, keepdims=True))
+            shrink = jnp.exp(before - top)
+            probs = jnp.exp(scores - top)
+            total = SUM[row, :] * shrink + jnp.sum(probs, axis=0, keepdims=True)
+            mixed = ACC[mix_at(hp, h)] * shrink + dot_nn(values[own], probs.astype(BF))
+            STAT[0, row, :] = top + jnp.log(total)
+            outs.append(mixed * (1.0 / total))
+        ATT[:, cols] = jnp.concatenate(outs, axis=0).T.astype(BF)
+        return carry
+
+    def again(rows, start):
+        unit, _ = norm_parts(TOK[rows, :].astype(F32))
+        ATT[rows, :] = (unit * fg + fs).astype(BF)
+
+    tiles(again)
+    padded_transpose(ATT, XN)
+
+    for copy in down_load:
+        copy.wait()
+    for f in range(2):
+        ffn_load[f][1].wait()
+
+    def early_step(rows, start):
+        dout = COT[rows, :]
+        block = start // TILE * 2
+
+        def keep(f, lo, value):
+            CH[f, 0, pl.ds(block, 2), :, :, :, lo : lo + value.shape[1]] = value.astype(BF).reshape(
+                2, 4, 2, 16, value.shape[1]
+            )
+
+        for f in range(2):
+            keep(f, 0, dot_nt(dout, W[6 + f]))
+        keep(2, 0, dot_nt(dout, SEC[...]))
+        middle = dot_nt(dout, ACT[...])
+        keep(2, 512, middle[:, 0:256])
+        keep(3, 0, middle[:, 256:512])
+        keep(3, 256, dot_nt(dout, DH[...]))
+
+    tiles(early_step)
+
+    far_tokens.wait_recv()
+    tiles(projection(FT, QF, KF, VF))
+    lax.fori_loop(0, 6, attend_far, 0)
 
     w_load[3].wait()
 
@@ -563,23 +614,24 @@
         ACC2[rows, :] = jnp.zeros((TILE, WIDTH), F32)
 
     tiles(out_step)
-    padded_transpose(SEC)
+    padded_transpose(SEC, XT)
     VS[0] = jnp.zeros((16, WIDTH), F32)
 
     for f in range(4):
         slot = f % 2
-        for copy in ffn_load[f]:
-            copy.wait()
+        ffn_load[f][0].wait()
+        if f > 1:
+            ffn_load[f][1].wait()
         ub = ub_ref[WIDTH * f : WIDTH * (f + 1)].reshape(1, WIDTH)
 
-        def ffn_step(rows, start, slot=slot, ub=ub):
-            dout = COT[rows, :]
+        def ffn_step(rows, start, f=f, slot=slot, ub=ub):
+            early = CH[f, 0, pl.ds(start // TILE * 2, 2)].reshape(TILE, WIDTH).astype(F32)
             hidden = dot_nn(SEC[rows, :], W[4 + slot]) + ub
             cdf = 0.5 * (1.0 + lax.erf(hidden * 0.7071067811865476))
             density = jnp.exp(-0.5 * hidden * hidden) * 0.3989422804014327
             active = (hidden * cdf).astype(BF)
             ACT[rows, :] = active
-            dhidden = (dot_nt(dout, W[6 + slot]) * (cdf + hidden * density)).astype(BF)
+            dhidden = (early * (cdf + hidden * density)).astype(BF)
             DH[rows, :] = dhidden
             ACC1[rows, :] += dot_nn(active, W[6 + slot])
             ACC2[rows, :] += dot_nt(dhidden, W[4 + slot])
@@ -602,7 +654,6 @@
         if f >= 1:
             rs_first(f - 1)
 
-    rs_mid(1)
     for k in range(3):
         rs_core(4 + k)
 
@@ -634,7 +685,6 @@
             remote(DH.at[:, half], FDO.at[:, half], xsend.at[2 + r], xrecv.at[2 + r], partner)
         )
     rs_first(3)
-    rs_second(0)
     VS[0, 7:8, :] = row_sum(COT[...])
     VS[0, 2:3, :] = row_sum(SEC[...])
 
@@ -646,14 +696,13 @@
     STAT[1] = dot_nt(in_head, rough) + dot_nt(in_head, (product - rough.astype(F32)).astype(BF))
     far_stats = remote(STAT, FSTAT, xsend.at[4], xrecv.at[4], partner)
 
-    padded_transpose(ATT)
+    padded_transpose(ATT, XT)
     gone((0, 0, 0))
     chunk_matmul(7, lambda: SEC[...])
     rs_core(7)
     rs_first(4)
-    rs_mid(2)
-    rs_second(1)
     rs_first(5)
+    rs_mid(1)
 
     def own_queries(hp, carry):
         cols = pair_cols(hp)
@@ -690,27 +739,30 @@
         return carry
 
     lax.fori_loop(0, 2, own_queries, 0)
-    rs_mid(3)
     rs_first(6)
+    rs_mid(2)
+    rs_second(0)
     lax.fori_loop(2, 4, own_queries, 0)
     rs_first(7)
+    rs_mid(3)
+    rs_second(1)
     rs_mid(4)
+    lax.fori_loop(4, 6, own_queries, 0)
     rs_mid(5)
     rs_second(2)
     rs_third(0)
-    rs_third(1)
-    lax.fori_loop(4, 6, own_queries, 0)
-    rs_mid(6)
-    rs_second(3)
-    rs_second(4)
-    rs_third(2)
 
     def again(rows, start):
         unit, _ = norm_parts(TOK[rows, :].astype(F32))
         ATT[rows, :] = (unit * fg + fs).astype(BF)
 
-    tiles(again)
-    padded_transpose(ATT)
+
+    gone((1, 0, 0))
+    chunk_matmul(8, lambda: QO[...])
+    rs_core(8)
+    rs_mid(6)
+    rs_second(3)
+    rs_third(1)
 
     far_stats.wait_recv()
 
@@ -735,41 +787,38 @@
         VO[:, cols] = dv.astype(BF)
         return carry
 
-    for j in range(3):
-        c = 8 + j
-        if j < 2:
-            far_dout[j].wait_recv()
-        lax.fori_loop(2 * j, 2 * j + 2, far_queries, 0)
+    def chunk_in(c, joined):
         gone((c - 7, 0, 0))
-        cols = slice(TILE * j, TILE * (j + 1))
-
-        def joined(cols=cols):
-            return jnp.concatenate([QO[:, cols], KO[:, cols], VO[:, cols]], axis=1)
-
         chunk_matmul(c, joined)
         rs_core(c)
-        if j == 0:
-            rs_mid(7)
-            rs_second(5)
-            rs_second(6)
-            rs_third(3)
-            rs_third(4)
-            rs_fourth(0)
-            rs_fourth(1)
-        if j == 1:
-            rs_first(8)
-            rs_second(7)
-            rs_third(5)
-            rs_third(6)
-            rs_fourth(2)
-            rs_fourth(3)
-            rs_end(0)
-        if j == 2:
-            rs_first(9)
-            rs_mid(8)
-            rs_third(7)
-            rs_fourth(4)
-            rs_fourth(5)
+
+    def keys_values(j):
+        cols = slice(384 * j, 384 * (j + 1))
+        return jnp.concatenate([KO[:, cols], VO[:, cols]], axis=1)
+
+    far_dout[0].wait_recv()
+    lax.fori_loop(0, 3, far_queries, 0)
+    chunk_in(9, lambda: keys_values(0))
+    rs_first(8)
+    rs_mid(7)
+    rs_second(4)
+    rs_second(5)
+    rs_third(2)
+    rs_third(3)
+    rs_fourth(0)
+    far_dout[1].wait_recv()
+    lax.fori_loop(3, 4, far_queries, 0)
+    rs_first(9)
+    lax.fori_loop(4, 6, far_queries, 0)
+    chunk_in(10, lambda: keys_values(1))
+    rs_mid(8)
+    rs_second(6)
+    rs_second(7)
+    rs_third(4)
+    rs_third(5)
+    rs_fourth(1)
+    rs_fourth(2)
+    rs_fourth(3)
 
     VS[0, 0:1, :] = row_sum(QO[...])
     VS[0, 1:2, :] = row_sum(VO[...])
@@ -789,8 +838,7 @@
         ) * inverse
         TOK[rows, :] = (RES[rows, :] + through).astype(BF)
 
-    for copy in far_tokens:
-        copy.wait_send()
+    far_tokens.wait_send()
     tiles(first_back)
     gt_store = load(TOK, gt_hbm, iosem.at[3])
 
@@ -813,34 +861,33 @@
     rs_first(10)
     rs_mid(9)
     rs_second(8)
-    rs_fourth(6)
-    rs_fourth(7)
+    rs_third(6)
+    rs_third(7)
+    rs_fourth(4)
+    rs_fourth(5)
     vec_add(0)
     vec_send(1, z_peer[1:])
     rs_mid(10)
     rs_second(9)
     rs_third(8)
+    rs_fourth(6)
+    rs_second(10)
     vec_add(1)
     vec_send(2, x_peer[1:])
-    rs_second(10)
     rs_third(9)
+    rs_fourth(7)
     rs_fourth(8)
+    rs_third(10)
     vec_add(2)
     vec_send(3, y_peer[1:])
-    rs_third(10)
+    rs_end(0)
     rs_fourth(9)
     rs_fourth(10)
     vec_add(3)
-    rs_end(10)
-
-    spot = lax.broadcasted_iota(jnp.int32, (WIDTH, 128), 0)
-    lane = lax.broadcasted_iota(jnp.int32, (WIDTH, 128), 1)
-    narrow = jnp.where((lane < 12) & (spot == lane + 12 * dp), 1.0, 0.0)
-    wide = jnp.where((lane < 48) & (spot == lane + 48 * (dp % 16)), 1.0, 0.0)
+
     vectors = VS[4]
-    exact = dict(precision=lax.Precision.HIGHEST, preferred_element_type=F32)
-    small = jnp.dot(vectors, narrow, **exact)
-    large = jnp.dot(vectors, wide, **exact)
+    small = pltpu.roll(vectors, (WIDTH - 12 * dp) % WIDTH, 1)
+    large = pltpu.roll(vectors, (WIDTH - 48 * (dp % 16)) % WIDTH, 1)[:, 0:128]
     row = lax.broadcasted_iota(jnp.int32, (16, 128), 0)
     large = jnp.sum(jnp.where(row == 8 + dp // 16, large, 0.0), axis=0, keepdims=True)
     for i, ref in enumerate(
@@ -862,9 +909,24 @@
 
 
 def finish(*refs):
-    count = len(refs) // 2
+    count = (len(refs) - 2) // 3
+    sems = refs[3 * count :]
+    hops = []
     for i in range(count):
-        refs[count + i][...] = refs[i][...]
+        src, dst, held = refs[i], refs[count + i], refs[2 * count + i]
+        hops.append(
+            (
+                pltpu.make_async_copy(src, held, sems[0].at[i]),
+                pltpu.make_async_copy(held, dst, sems[1].at[i]),
+            )
+        )
+    for first, _ in hops:
+        first.start()
+    for first, second in hops:
+        first.wait()
+        second.start()
+    for _, second in hops:
+        second.wait()
 
 
 def body(
@@ -922,13 +984,13 @@
             pltpu.VMEM((8, WIDTH, WIDTH), BF),
             pltpu.VMEM((SLOTS, 2, 4, 4, 2, 16, WIDTH), BF),
             pltpu.VMEM((CHUNKS, 2, 4, 4, 16, WIDTH), BF),
-            pltpu.VMEM((CHUNKS, 3, 2, 4, 16, WIDTH), BF),
-            pltpu.VMEM((CHUNKS, 3, 2, 16, WIDTH), BF),
-            pltpu.VMEM((CHUNKS, 3, 16, WIDTH), BF),
-            pltpu.VMEM((2, 3, 4, 4, 16, 384), BF),
-            pltpu.VMEM((2, 3, 4, 16, 384), BF),
-            pltpu.VMEM((2, 3, 16, 384), BF),
-            pltpu.VMEM((2, 2, 16, 384), F32),
+            pltpu.VMEM((CHUNKS - len(Y_FIRST), 3, 2, 4, 16, WIDTH), BF),
+            pltpu.VMEM((CHUNKS - len(Y_FIRST), 3, 2, 16, WIDTH), BF),
+            pltpu.VMEM((CHUNKS - len(Y_FIRST), 3, 16, WIDTH), BF),
+            pltpu.VMEM((1, 3, 4, 4, 16, 384), BF),
+            pltpu.VMEM((1, 3, 4, 16, 384), BF),
+            pltpu.VMEM((1, 3, 16, 384), BF),
+            pltpu.VMEM((1, 2, 16, 384), F32),
             block(BF),
             block(BF),
             pltpu.VMEM((2, 16, ROWS), F32),
@@ -936,6 +998,7 @@
         ]
         + [block(BF)] * 12
         + [
+            pltpu.VMEM((1024, ROWS), BF),
             pltpu.VMEM((1024, ROWS), BF),
             block(F32),
             block(F32, 2),
@@ -946,6 +1009,7 @@
             pltpu.VMEM((5, 16, WIDTH), F32),
             pltpu.VMEM((10, 16, WIDTH), F32),
             pltpu.SemaphoreType.DMA((8,)),
+            pltpu.SemaphoreType.DMA((3,)),
             pltpu.SemaphoreType.DMA((4,)),
             pltpu.SemaphoreType.DMA((5,)),
             pltpu.SemaphoreType.DMA((5,)),
@@ -980,8 +1044,10 @@
     return pl.pallas_call(
         finish,
         out_shape=tuple(jax.ShapeDtypeStruct(value.shape, value.dtype) for value in out),
-        in_specs=[vmem] * len(out),
-        out_specs=(vmem,) * len(out),
+        in_specs=[hbm] * len(out),
+        out_specs=(hbm,) * len(out),
+        scratch_shapes=[pltpu.VMEM(value.shape, value.dtype) for value in out]
+        + [pltpu.SemaphoreType.DMA((len(out),))] * 2,
         name="finish",
     )(*out)
 

time: 136 us -> 131 us (0.963)
  Pallas kernels: 135 us -> 130 us
    pallas_call x1, Pallas kernels: 132 us -> 127 us  [body(): pl.pallas_call(kernel, out_shape=(rows, rows, f32(12, 3 * WIDTH), f32(12)...]
where the time goes in v1:
time: 131 us
  Pallas kernels  130 us (99%)
    pallas_call x1, Pallas kernels, body(): pl.pallas_call(kernel, out_shape=(rows, rows, f32(12, 3 * WIDTH), f32(12)...  127 us
    pallas_call x1, Pallas kernels, body(): pl.pallas_call(finish, out_shape=tuple((jax.ShapeDtypeStruct(value.shape,...  2.76 us

profile of v1, /device:TPU:0, one launch (start us, length us, event | category | flops | bytes accessed | tf_op | source)
XLA Modules:
  0.0 131.0 jit_solution(10988704475973420927)
XLA Ops:
  0.7 127.4 %encoder.1 = (bf16[512,768]{1,0:T(8,128)(2,1)}, bf16[512,768]{1,0:T(8,128)(2,1)}, f32[12,2304]{1,0:T(8,128)}, f32[12]{0:T(128)}, f32[12]{0:T(128)}, /*index=5*/f...) custom-call(s32[1,2]{1,0:T(1,128)} %counts_ref.1, ...), custom_call_target="tpu_custom_call" | custom-call | tf_op jit(solution)/shard_map/encoder/pallas_call | solution.py:962
  128.1 2.8 %finish.1 = (bf16[512,768]{1,0:T(8,128)(2,1)}, bf16[512,768]{1,0:T(8,128)(2,1)}, f32[12,2304]{1,0:T(8,128)}, f32[12]{0:T(128)}, f32[12]{0:T(128)}, /*index=5*/f3...) custom-call(bf16[512,768]{1,0:T(8,128)(2,1)} %get-tuple-element.30.r, ...), custom_call_target="tpu_custom_call" | custom-call | tf_op jit(solution)/shard_map/finish/pallas_call | solution.py:1044

commit v2 on v1

--- a/solution.py
+++ b/solution.py
@@ -23,7 +23,7 @@
     ((0, 0, 768),),
     ((1, 0, 768),),
     ((0, 0, 768),),
-    ((1, 0, 768),),
+    ((0, 0, 384), (1, 384, 768)),
     ((0, 0, 384), (1, 384, 768)),
     ((3, 0, 384), (4, 384, 768)),
 )
@@ -467,15 +467,15 @@
             ).astype(BF)
 
     def chunk_matmul(c, right):
+        left = XT if c < 8 else XN
+
         def block(m, carry):
-            start = pl.multiple_of(m * TILE, TILE)
-            out = dot_nn((XT if c < 8 else XN)[pl.ds(start, TILE), :], right())
-            CH[c % SLOTS, m // 2, pl.ds(2 * (m % 2), 2)] = out.astype(BF).reshape(
-                2, 4, 2, 16, WIDTH
-            )
+            cols = pl.ds(pl.multiple_of(m * TILE, TILE), TILE)
+            out = dot_nn(left[...], right[:, cols]).astype(BF)
+            CH[c % SLOTS, :, :, :, :, :, cols] = out.reshape(2, 4, 4, 2, 16, TILE)
             return carry
 
-        lax.fori_loop(0, 4, block, 0)
+        lax.fori_loop(0, 3, block, 0)
 
     ones = jnp.ones((16, ROWS), BF)
 
@@ -639,7 +639,9 @@
         tiles(ffn_step)
         if f + 2 < 4:
             ffn_load[f + 2] = load_ffn(f + 2)
-        chunk_matmul(f, lambda: DH[...])
+        if f >= 1:
+            rs_first(f - 1)
+        chunk_matmul(f, DH)
         rs_core(f)
         VS[0, 8 + f : 9 + f, :] = row_sum(DH[...])
 
@@ -651,9 +653,6 @@
             return carry
 
         lax.fori_loop(0, 2, down_step, 0)
-        if f >= 1:
-            rs_first(f - 1)
-
     for k in range(3):
         rs_core(4 + k)
 
@@ -698,7 +697,7 @@
 
     padded_transpose(ATT, XT)
     gone((0, 0, 0))
-    chunk_matmul(7, lambda: SEC[...])
+    chunk_matmul(7, SEC)
     rs_core(7)
     rs_first(4)
     rs_first(5)
@@ -758,7 +757,7 @@
 
 
     gone((1, 0, 0))
-    chunk_matmul(8, lambda: QO[...])
+    chunk_matmul(8, QO)
     rs_core(8)
     rs_mid(6)
     rs_second(3)
@@ -787,18 +786,17 @@
         VO[:, cols] = dv.astype(BF)
         return carry
 
-    def chunk_in(c, joined):
+    def chunk_in(c):
+        cols = slice(384 * (c - 9), 384 * (c - 8))
+        ACT[:, 0:384] = KO[:, cols]
+        ACT[:, 384:768] = VO[:, cols]
         gone((c - 7, 0, 0))
-        chunk_matmul(c, joined)
+        chunk_matmul(c, ACT)
         rs_core(c)
-
-    def keys_values(j):
-        cols = slice(384 * j, 384 * (j + 1))
-        return jnp.concatenate([KO[:, cols], VO[:, cols]], axis=1)
 
     far_dout[0].wait_recv()
     lax.fori_loop(0, 3, far_queries, 0)
-    chunk_in(9, lambda: keys_values(0))
+    chunk_in(9)
     rs_first(8)
     rs_mid(7)
     rs_second(4)
@@ -810,7 +808,7 @@
     lax.fori_loop(3, 4, far_queries, 0)
     rs_first(9)
     lax.fori_loop(4, 6, far_queries, 0)
-    chunk_in(10, lambda: keys_values(1))
+    chunk_in(10)
     rs_mid(8)
     rs_second(6)
     rs_second(7)

time: 131 us -> 129 us (0.985)
  Pallas kernels: 130 us -> 128 us
    pallas_call x1, Pallas kernels: 127 us -> 125 us  [body(): pl.pallas_call(kernel, out_shape=(rows, rows, f32(12, 3 * WIDTH), f32(12)...]
where the time goes in v2:
time: 129 us
  Pallas kernels  128 us (99%)
    pallas_call x1, Pallas kernels, body(): pl.pallas_call(kernel, out_shape=(rows, rows, f32(12, 3 * WIDTH), f32(12)...  125 us
    pallas_call x1, Pallas kernels, body(): pl.pallas_call(finish, out_shape=tuple((jax.ShapeDtypeStruct(value.shape,...  2.76 us

profile of v2, /device:TPU:0, one launch (start us, length us, event | category | flops | bytes accessed | tf_op | source)
XLA Modules:
  0.0 129.0 jit_solution(843081905435307343)
XLA Ops:
  0.7 125.4 %encoder.1 = (bf16[512,768]{1,0:T(8,128)(2,1)}, bf16[512,768]{1,0:T(8,128)(2,1)}, f32[12,2304]{1,0:T(8,128)}, f32[12]{0:T(128)}, f32[12]{0:T(128)}, /*index=5*/f...) custom-call(s32[1,2]{1,0:T(1,128)} %counts_ref.1, ...), custom_call_target="tpu_custom_call" | custom-call | tf_op jit(solution)/shard_map/encoder/pallas_call | solution.py:960
  126.0 2.8 %finish.1 = (bf16[512,768]{1,0:T(8,128)(2,1)}, bf16[512,768]{1,0:T(8,128)(2,1)}, f32[12,2304]{1,0:T(8,128)}, f32[12]{0:T(128)}, f32[12]{0:T(128)}, /*index=5*/f3...) custom-call(bf16[512,768]{1,0:T(8,128)(2,1)} %get-tuple-element.30.r, ...), custom_call_target="tpu_custom_call" | custom-call | tf_op jit(solution)/shard_map/finish/pallas_call | solution.py:1042

commit v3 on v2

--- a/solution.py
+++ b/solution.py
@@ -22,7 +22,7 @@
     ((1, 0, 768),),
     ((0, 0, 768),),
     ((1, 0, 768),),
-    ((0, 0, 768),),
+    ((0, 0, 384), (1, 384, 768)),
     ((0, 0, 384), (1, 384, 768)),
     ((0, 0, 384), (1, 384, 768)),
     ((3, 0, 384), (4, 384, 768)),

time: 129 us -> 128 us (level)
  no operation moved by 1% of the time
where the time goes in v3:
time: 128 us
  Pallas kernels  127 us (99%)
    pallas_call x1, Pallas kernels, body(): pl.pallas_call(kernel, out_shape=(rows, rows, f32(12, 3 * WIDTH), f32(12)...  124 us
    pallas_call x1, Pallas kernels, body(): pl.pallas_call(finish, out_shape=tuple((jax.ShapeDtypeStruct(value.shape,...  2.76 us

profile of v3, /device:TPU:0, one launch (start us, length us, event | category | flops | bytes accessed | tf_op | source)
XLA Modules:
  0.0 128.0 jit_solution(17944207040018897021)
XLA Ops:
  0.7 124.4 %encoder.1 = (bf16[512,768]{1,0:T(8,128)(2,1)}, bf16[512,768]{1,0:T(8,128)(2,1)}, f32[12,2304]{1,0:T(8,128)}, f32[12]{0:T(128)}, f32[12]{0:T(128)}, /*index=5*/f...) custom-call(s32[1,2]{1,0:T(1,128)} %counts_ref.1, ...), custom_call_target="tpu_custom_call" | custom-call | tf_op jit(solution)/shard_map/encoder/pallas_call | solution.py:960
  125.0 2.8 %finish.1 = (bf16[512,768]{1,0:T(8,128)(2,1)}, bf16[512,768]{1,0:T(8,128)(2,1)}, f32[12,2304]{1,0:T(8,128)}, f32[12]{0:T(128)}, f32[12]{0:T(128)}, /*index=5*/f3...) custom-call(bf16[512,768]{1,0:T(8,128)(2,1)} %get-tuple-element.30.r, ...), custom_call_target="tpu_custom_call" | custom-call | tf_op jit(solution)/shard_map/finish/pallas_call | solution.py:1042

commit v4 on v3

--- a/solution.py
+++ b/solution.py
@@ -817,6 +817,7 @@
     rs_fourth(1)
     rs_fourth(2)
     rs_fourth(3)
+    rs_mid(9)
 
     VS[0, 0:1, :] = row_sum(QO[...])
     VS[0, 1:2, :] = row_sum(VO[...])
@@ -857,7 +858,6 @@
 
     vec_send(0, [sibling])
     rs_first(10)
-    rs_mid(9)
     rs_second(8)
     rs_third(6)
     rs_third(7)

time: 128 us -> 128 us (level)
  no operation moved by 1% of the time
where the time goes in v4:
time: 128 us
  Pallas kernels  127 us (99%)
    pallas_call x1, Pallas kernels, body(): pl.pallas_call(kernel, out_shape=(rows, rows, f32(12, 3 * WIDTH), f32(12)...  124 us
    pallas_call x1, Pallas kernels, body(): pl.pallas_call(finish, out_shape=tuple((jax.ShapeDtypeStruct(value.shape,...  2.76 us

profile of v4, /device:TPU:0, one launch (start us, length us, event | category | flops | bytes accessed | tf_op | source)
XLA Modules:
  0.0 128.0 jit_solution(16146376685171314638)
XLA Ops:
  0.7 124.4 %encoder.1 = (bf16[512,768]{1,0:T(8,128)(2,1)}, bf16[512,768]{1,0:T(8,128)(2,1)}, f32[12,2304]{1,0:T(8,128)}, f32[12]{0:T(128)}, f32[12]{0:T(128)}, /*index=5*/f...) custom-call(s32[1,2]{1,0:T(1,128)} %counts_ref.1, ...), custom_call_target="tpu_custom_call" | custom-call | tf_op jit(solution)/shard_map/encoder/pallas_call | solution.py:960
  125.0 2.8 %finish.1 = (bf16[512,768]{1,0:T(8,128)(2,1)}, bf16[512,768]{1,0:T(8,128)(2,1)}, f32[12,2304]{1,0:T(8,128)}, f32[12]{0:T(128)}, f32[12]{0:T(128)}, /*index=5*/f3...) custom-call(bf16[512,768]{1,0:T(8,128)(2,1)} %get-tuple-element.30.r, ...), custom_call_target="tpu_custom_call" | custom-call | tf_op jit(solution)/shard_map/finish/pallas_call | solution.py:1042
